TPU v7x, 512 devices: a whole 4x8x8 slice. The times are simulated.
512 devices in a mesh: dp: 8 (over z), seq: 64 (over x, y, core).
Axes of the slice: x: 4, y: 8, z: 8, core: 2. Of those that a mesh axis runs over, the one named last changes fastest.
Arguments:
- inputs: bfloat16 [8, 8192, 512], P('dp', 'seq'), may hold values from -16 to 16
- weight: bfloat16 [512, 2048], P(('dp', 'seq')), may hold values from -0.25 to 0.25
- table: bfloat16 [4096, 1024], P('dp'), may hold values from -1.5 to 1.5
- grad_out: bfloat16 [8, 16384, 512], P('dp', 'seq'), may hold values from -6 to 6
- clip_speaker: int32 [8], P('dp'), may hold values from 0 to 4095
- part_speaker: int32 [8, 64], P('dp', 'seq'), may hold values from 0 to 4095
- quote_bounds: int32 [8, 64, 2], P('dp', 'seq'), may hold values from 0 to 255, as said below
Outputs:
- grad_inputs: bfloat16 [8, 8192, 512], P('dp', 'seq')
- grad_weight: float32 [512, 2048], P(('dp', 'seq'))
- grad_table: bfloat16 [4096, 1024], P('dp')
Inputs may be any that keep to these rules, and one draw needn't show every extreme that they name: `quote_bounds`: each span's quoted segment is at least 32 and at most 128 frames long and lies inside the span.
All inputs are finite; a program needn't handle non-finite values.
Results may differ from a plain program's by a relative error of at most 0.0049.
Values may be sent and summed in bfloat16 or wider, within the bound.
A program may use at most 64 MiB of HBM per device.

v0:
```python
import jax
import jax.numpy as jnp
from jax import lax
from jax.sharding import PartitionSpec as P


def padded(value, sides, width):
    for axis, dim in sides:
        peers, length = (lax.axis_size(axis), value.shape[dim])
        up = [(i, (i + 1) % peers) for i in range(peers - 1)]
        down = [(j, i) for i, j in up]
        last = lax.slice_in_dim(value, length - width, length, axis=dim)
        leading = lax.slice_in_dim(value, 0, width, axis=dim)
        before = lax.ppermute(last, axis, up)
        after = lax.ppermute(leading, axis, down)
        value = jnp.concatenate([before, value, after], axis=dim)
    return value


def mish_grad(pre, cotangent):
    soft = jax.nn.softplus(pre)
    tangent = jnp.tanh(soft)
    return cotangent * (tangent + pre * jax.nn.sigmoid(pre) * (1.0 - tangent * tangent))


def owned_rows(values, speakers, own_count):
    local = speakers - lax.axis_index("dp") * own_count
    picker = (jnp.arange(own_count, dtype=jnp.int32)[:, None] == local[None, :]).astype(jnp.float32)
    return jnp.dot(
        picker, values, precision=lax.Precision.HIGHEST, preferred_element_type=jnp.float32
    )


def body(inputs, weight, table, grad_out, clip_speaker, part_speaker, quote_bounds):
    frames_in = inputs[0]
    cotangent = grad_out[0].astype(jnp.float32)
    frame_count = frames_in.shape[0]
    width = frames_in.shape[1]
    out_count = 2 * frame_count
    own_count = table.shape[0]
    wanted = jnp.concatenate([clip_speaker, part_speaker[0, 0:1]])
    asked = lax.all_gather(wanted, "dp", axis=0, tiled=True)
    local_ids = asked - lax.axis_index("dp") * own_count
    picker = (local_ids[:, None] == jnp.arange(own_count, dtype=jnp.int32)[None, :]).astype(
        jnp.bfloat16
    )
    served = jnp.dot(picker, table, preferred_element_type=jnp.float32).astype(jnp.bfloat16)
    replies = lax.all_to_all(served, "dp", split_axis=0, concat_axis=0, tiled=True)
    film_rows = jnp.sum(replies.astype(jnp.float32).reshape(-1, 2, 2 * width), 0)
    source = padded(frames_in, (("seq", 0),), 1)
    full_weight = lax.all_gather(weight, ("dp", "seq"), axis=0, tiled=True)
    products = jnp.dot(source, full_weight, preferred_element_type=jnp.float32)
    middle = products[1:-1]
    tap_prev = products[:-2, 3 * width :]
    tap_next = products[2:, :width]
    even_out = middle[:, width : 2 * width] + tap_prev
    odd_out = middle[:, 2 * width : 3 * width] + tap_next
    upsampled = jnp.stack([even_out, odd_out], 1).reshape(out_count, width)
    position = jnp.arange(out_count, dtype=jnp.int32)
    quoted = ((position >= quote_bounds[0, 0, 0]) & (position < quote_bounds[0, 0, 1])).astype(
        jnp.float32
    )
    film = (1.0 - quoted)[:, None] * film_rows[0][None, :] + quoted[:, None] * film_rows[1][None, :]
    scale_part = film[:, :width]
    shift_part = film[:, width:]
    pre = upsampled * (1.0 + scale_part) + shift_part
    grad_pre = mish_grad(pre, cotangent)
    grad_up = (grad_pre * (1.0 + scale_part)).astype(jnp.bfloat16)
    paired = grad_up.reshape(frame_count, 2 * width)
    edged = padded(paired, (("seq", 0),), 1)
    taps_grad = jnp.concatenate(
        [edged[:-2, width:], paired[:, :width], paired[:, width:], edged[2:, :width]], 1
    )
    grad_frames = lax.dot_general(
        taps_grad, full_weight, (((1,), (1,)), ((), ())), preferred_element_type=jnp.float32
    )
    wscale = 1.0 / jnp.sqrt(jnp.float32(lax.axis_size("dp") * lax.axis_size("seq") * frame_count))
    grad_weight = lax.psum_scatter(
        lax.dot_general(
            frames_in, taps_grad, (((0,), (0,)), ((), ())), preferred_element_type=jnp.float32
        )
        * wscale,
        ("dp", "seq"),
        scatter_dimension=0,
        tiled=True,
    )
    fscale = 1.0 / jnp.sqrt(jnp.float32(out_count))
    film_grad = jnp.concatenate([grad_pre * upsampled, grad_pre], 1) * fscale
    slots = jnp.stack([1.0 - quoted, quoted], 0)
    segment = jnp.dot(
        slots, film_grad, precision=lax.Precision.HIGHEST, preferred_element_type=jnp.float32
    )
    gathered, speakers = (
        lax.all_gather(segment, "dp", axis=0, tiled=True),
        lax.all_gather(wanted, "dp", axis=0, tiled=True),
    )
    table_sum = lax.psum(owned_rows(gathered, speakers, own_count), "seq")
    return (grad_frames.astype(jnp.bfloat16)[None], grad_weight, table_sum.astype(jnp.bfloat16))


def solution(mesh):
    placed = (
        P("dp", "seq", None),
        P(("dp", "seq"), None),
        P("dp", None),
        P("dp", "seq", None),
        P("dp"),
        P("dp", "seq"),
        P("dp", "seq", None),
    )
    return jax.shard_map(
        body,
        mesh=mesh,
        in_specs=placed,
        out_specs=(P("dp", "seq", None), P(("dp", "seq"), None), P("dp", None)),
        check_vma=False,
    )
```

profile of v0, /device:TPU:1, one launch (start us, length us, event | category | flops | bytes accessed | tf_op | source)
XLA Modules:
  0.0 459.1 jit_solution(11151766312970458424)
XLA Ops:
  7.2 0.0 copy-start
  7.2 0.0 all-gather.4.cloned.1.call-start
  7.2 0.7 all-gather.4.cloned.1.call-update
  7.9 0.7 slice_bitcast_fusion.3
  8.6 8.8 %collective-permute-start.1 = (bf16[1,512]{1,0:T(2,128)(2,1)S(1)}, bf16[1,512]{1,0:T(2,128)(2,1)S(1)}, u32[]{:S(2)}, u32[]{:S(2)}) collective-permute-start(bf16[1,512]{1,0:T(2,128)(2,1)S(1)} %get-tuple-element.19), channel_id=1, source_target_pairs={{1,0},{2,1},{3,2},{4,3},{5,4},{6,5},{7,6},{8,7},{9,8},{10,9},{11,1... | collective-permute-start | bytes 3080 | tf_op jit(solution)/shard_map/ppermute | solution.py:15
  17.4 1.9 collective-permute-start
  20.6 1.3 dynamic-slice
  22.6 0.2 add_dynamic-update-slice_fusion
  22.8 12.1 %all-reduce = s32[16]{0:T(128)S(1)} all-reduce(s32[16]{0:T(128)S(1)} %add_dynamic-update-slice_fusion), channel_id=1, replica_groups=mesh['dp'=8,'seq'=64] {'dp'}, use_global_device_ids=true, to_apply=%add | all-reduce | flops 16 | bytes 128
  34.9 0.0 copy-done
  34.9 0.3 convolution_convert_fusion
  35.2 0.6 all_to_all.6
  35.8 3.3 all-to-all-start
  39.2 0.0 all-reduce.5.cloned.1.call-start
  39.2 1.3 fusion.41
  40.5 1.2 and_convert_fusion.1
  41.7 1.2 broadcast_subtract_fusion.1
  42.9 3.0 all-to-all-done
  46.0 0.2 multiply_add_fusion
  46.2 0.0 copy-start.4
  46.2 0.0 collective-permute-done.1
  46.2 0.0 collective-permute-done
  46.2 90.5 %all-gather.4.cloned.1.call-done = bf16[512,1,2048]{2,1,0:T(2,128)(2,1)} async-done(((bf16[1,1,2048]{2,1,0:T(2,128)(2,1)}), bf16[512,1,2048]{2,1,0:T(2,128)(2,1)}) %all-gather.4.cloned.1.call-update) | async-done | bytes 2097168 | tf_op jit(solution)/shard_map/all_gather | solution.py:51
  136.8 3.7 fusion.2
  140.5 0.1 fusion.19
  140.6 0.0 copy-start.3
  140.6 0.4 copy.13
  141.0 1.2 reshape.57
  142.2 0.0 copy-done.4
  142.2 1.6 fusion.39
  143.8 0.1 multiply_convert_fusion
  143.9 2.2 collective-permute-start.3
  146.1 3.4 collective-permute-start.2
  149.5 0.1 reshape.58
  149.6 0.0 copy-start.1
  149.6 0.0 collective-permute-done.3
  149.7 0.6 collective-permute-done.2
  150.3 0.0 copy-done.3
  150.3 2.7 multiply_bitcast_fusion
  153.0 0.0 all-reduce.5.cloned.1.call-update
  153.0 0.0 copy-done.1
  153.0 0.0 copy-start.2
  153.0 1.3 and_convert_fusion
  154.3 1.2 broadcast_subtract_fusion
  155.5 0.6 convolution_bitcast_fusion
  156.1 19.2 %all-gather.1 = f32[8,2,1024]{2,1,0:T(2,128)S(1)} all-gather(f32[1,2,1024]{2,1,0:T(2,128)S(1)} %convolution_bitcast_fusion), channel_id=1, replica_groups=mesh['dp'=8,'seq'=64] {'dp'}, dimensions={0}, use_global_device_ids=true | all-gather | bytes 73728 | tf_op jit(solution)/shard_map/all_gather | solution.py:94
  175.4 1.0 fusion.20
  176.3 269.3 %all-reduce.6 = bf16[512,1024]{1,0:T(8,128)(2,1)} all-reduce(f32[512,1024]{1,0:T(8,128)S(1)} %fusion.20), channel_id=1, replica_groups=mesh['dp'=8,'seq'=64] {'seq'}, use_global_device_ids=true, to_apply=%region_2.3 | all-reduce | flops 524288 | bytes 3145728 | tf_op jit(solution)/shard_map/psum | solution.py:97
  445.6 0.0 copy-done.2
  445.6 4.2 fusion.7
  449.8 0.0 all-reduce.5.cloned.1.call-done
  449.8 1.6 constant_dynamic-slice_fusion
  451.4 0.9 copy.14
  (9 shorter events, 0.2 us)
Async XLA Ops:
  7.2 27.7 %copy-start = (bf16[512,1024]{1,0:T(8,128)(2,1)S(1)}, bf16[512,1024]{1,0:T(8,128)(2,1)}, u32[]{:S(2)}) copy-start(bf16[512,1024]{1,0:T(8,128)(2,1)} %param.9) | copy-start | bytes 3145732
  7.2 129.6 %all-gather.4.cloned.1.call-start = ((), (), s32[]{:S(2)}) async-start(), calls=%async_computation.1 | async-start | bytes 4202496 | tf_op jit(solution)/shard_map/all_gather | solution.py:51
  8.6 37.6 %collective-permute-start.1 = (bf16[1,512]{1,0:T(2,128)(2,1)S(1)}, bf16[1,512]{1,0:T(2,128)(2,1)S(1)}, u32[]{:S(2)}, u32[]{:S(2)}) collective-permute-start(bf16[1,512]{1,0:T(2,128)(2,1)S(1)} %get-tuple-element.19), channel_id=1, source_target_pairs={{1,0},{2,1},{3,2},{4,3},{5,4},{6,5},{7,6},{8,7},{9,8},{10,9},{11,1... | collective-permute-start | bytes 3080 | tf_op jit(solution)/shard_map/ppermute | solution.py:15
  17.4 28.8 %collective-permute-start = (bf16[1,512]{1,0:T(2,128)(2,1)S(1)}, bf16[1,512]{1,0:T(2,128)(2,1)S(1)}, u32[]{:S(2)}, u32[]{:S(2)}) collective-permute-start(bf16[1,512]{1,0:T(2,128)(2,1)S(1)} %get-tuple-element.18), channel_id=1, source_target_pairs={{0,1},{1,2},{2,3},{3,4},{4,5},{5,6},{6,7},{7,8},{8,9},{9,10},{10,1... | collective-permute-start | bytes 3080 | tf_op jit(solution)/shard_map/ppermute | solution.py:14
  35.8 10.2 %all-to-all-start = ((bf16[8,2,1024]{2,1,0:T(2,128)(2,1)}), bf16[8,2,1024]{2,1,0:T(2,128)(2,1)S(1)}, u32[]{:S(2)}, u32[]{:S(2)}) async-start(bf16[8,2,1024]{2,1,0:T(2,128)(2,1)} %all_to_all.6), calls=%async_computation | async-start | bytes 65536 | tf_op jit(solution)/shard_map/all_to_all | solution.py:48
  39.2 410.6 %all-reduce.5.cloned.1.call-start = ((), (), s32[]{:S(2)}) async-start(), calls=%async_computation.2 | async-start | bytes 8388608
  46.2 96.0 %copy-start.4 = (bf16[1,256,512]{2,1,0:T(8,128)(2,1)S(1)}, bf16[1,256,512]{2,1,0:T(8,128)(2,1)}, u32[]{:S(2)}) copy-start(bf16[1,256,512]{2,1,0:T(8,128)(2,1)} %param.10) | copy-start | bytes 786436
  140.6 9.7 %copy-start.3 = (bf16[1,128,512]{2,1,0:T(8,128)(2,1)S(1)}, bf16[1,128,512]{2,1,0:T(8,128)(2,1)}, u32[]{:S(2)}) copy-start(bf16[1,128,512]{2,1,0:T(8,128)(2,1)} %param.7) | copy-start | bytes 393220
  143.9 5.7 %collective-permute-start.3 = (bf16[1,1024]{1,0:T(2,128)(2,1)S(1)}, bf16[1,1024]{1,0:T(2,128)(2,1)S(1)}, u32[]{:S(2)}, u32[]{:S(2)}) collective-permute-start(bf16[1,1024]{1,0:T(2,128)(2,1)S(1)} %bitcast.54), channel_id=1, source_target_pairs={{1,0},{2,1},{3,2},{4,3},{5,4},{6,5},{7,6},{8,7},{9,8},{10,9},{11,1... | collective-permute-start | bytes 6152 | tf_op jit(solution)/shard_map/ppermute | solution.py:15
  146.1 4.1 collective-permute-start.2
  149.6 3.4 copy-start.1
  153.0 292.6 %copy-start.2 = (bf16[128,1024]{1,0:T(8,128)(2,1)S(1)}, bf16[128,1024]{1,0:T(8,128)(2,1)}, u32[]{:S(2)}) copy-start(bf16[128,1024]{1,0:T(8,128)(2,1)} %copy-done.1) | copy-start | bytes 786436
Sparse Core Ops, SparseCore 0:
  12.2 124.5 all-gather.3
  153.1 285.9 all-reduce.4
where the time goes:
time: 462 us; the launch traced here: 459 us
  blocking collectives  301 us (65%)
  waiting for transfers between devices  94.9 us (21%)
  starting transfers between devices  19.7 us (4%)
  between operations  16.2 us (4%)
  matrix products  12.5 us (3%)
  local copies, waits for them, and re-layouts  8.19 us (2%)
  other arithmetic  7.14 us (2%)
    psum x1, blocking collectives, body(): table_sum = lax.psum(owned_rows(gathered, speakers, own_count), 'seq')  269 us
    all_gather x1, waiting for transfers between devices, body(): full_weight = lax.all_gather(weight, ('dp', 'seq'), axis=0, tiled=True)  90.5 us
    all_gather x1, blocking collectives, body(): lax.all_gather(segment, 'dp', axis=0, tiled=True)  19.2 us
    unnamed x1, blocking collectives  12.1 us
    ppermute x2, starting transfers between devices, padded(): after = lax.ppermute(leading, axis, down)  10.9 us
  transfers between devices with their start and end apart: 7, of which 3 were waited for; matrix products, arithmetic and copies ran while one was open for 3% of the time, Pallas kernels for 0%

commit v1 on v0

v1 whole, which is shorter than its diff:
```python
import jax
import jax.numpy as jnp
from jax import lax
from jax.experimental import pallas as pl
from jax.experimental.pallas import tpu as pltpu
from jax.sharding import PartitionSpec as P

MESH = pl.DeviceIdType.MESH
F32 = jnp.float32
BF16 = jnp.bfloat16

NX, NY, NZ = 4, 8, 8
G = 8
C = 512
ROWS = 128
LANES = 128

(TILE, IDZ, WZ, WY, FILM, IDY, GOUT, ROWY, ROWZ, GWY, GWZ, GWX, INP, HALO, PAIR, GID, GIX, EDGE, TAB) = range(19)
CHANNELS = 19


def iota(shape, dim):
    return lax.broadcasted_iota(jnp.int32, shape, dim)


def dot(a, b):
    return jnp.dot(a, b, preferred_element_type=F32)


def dot_nt(a, b):
    return lax.dot_general(a, b, (((1,), (1,)), ((), ())), preferred_element_type=F32)


def dot_tn(a, b):
    return lax.dot_general(a, b, (((0,), (0,)), ((), ())), preferred_element_type=F32)


def mish_slope(pre):
    t = jnp.exp(-jnp.abs(pre))
    positive = pre >= 0.0
    num = jnp.where(positive, 1.0 + 2.0 * t, t * (t + 2.0))
    rest = jnp.where(positive, 2.0 * t * t, 2.0)
    inv = 1.0 / (num + rest)
    tangent = num * inv
    gate = jnp.where(positive, 1.0, t) / (1.0 + t)
    return tangent + pre * gate * (rest * (2.0 * num + rest) * inv * inv)


def kernel(
    inp, w, tab, go, clip, part, qb, o_gi, o_gw, o_gt,
    tsend, tg, idz, idy, wy, tabv, frs, frr, flm, xg, hx, xs, gov, gsend, gg, p01, wcat, pickt,
    ub, gbuf, segs, c1r, yr, zr, gws, gwr, gz, gzr, gxs, gxr, pb, gis, gir, gi2, gix, esend, ed,
    ssem, rsem, lsem,
):
    z = lax.axis_index("dp")
    s = lax.axis_index("seq")
    x = s // 16
    y = (s // 2) % NY
    c = s % 2
    m = 2 * x + c
    side = 2 * c - 1

    def at(zz, xx, yy, cc):
        return (zz, xx * 16 + yy * 2 + cc)

    def gpeer(i):
        return at(z, i // 2, y, i % 2)

    def ypeer(i):
        return at(z, x, i, c)

    def zpeer(i):
        return at(i, x, y, c)

    def xpeer(i):
        return at(z, i, y, c)

    sibling = at(z, x, y, 1 - c)

    def hpeer(i):
        return at(z, i, (y + side + NY) % NY, 1 - c)

    def remote(src, dst, chan, ss, rs, dev):
        return pltpu.make_async_remote_copy(
            src_ref=src, dst_ref=dst, send_sem=ssem.at[chan, ss], recv_sem=rsem.at[chan, rs],
            device_id=dev, device_id_type=MESH,
        )

    pending = []

    def spread(chan, me, peer, src, dst, n=8):
        def desc(d):
            i = (me + d) % n
            return remote(src(i), dst, chan, d, d, peer(i))

        @pl.loop(1, n)
        def _(d):
            desc(d).start()

        def finish():
            @pl.loop(1, n)
            def _(d):
                desc(d).wait_send()

        pending.append(finish)

    def collect(chan, me, peer, slot, n=8):
        @pl.loop(1, n)
        def _(d):
            i = (me - d + n) % n
            remote(slot(i), slot(i), chan, d, d, peer(i)).wait_recv()

    xcol = pl.multiple_of(x * LANES, LANES)
    scol = pl.multiple_of(C + x * LANES, LANES)
    get_go = pltpu.make_async_copy(go.at[0], gov, lsem.at[0])
    get_in = pltpu.make_async_copy(inp.at[0], xg.at[m], lsem.at[1])
    get_scale = pltpu.make_async_copy(tab.at[:, pl.ds(xcol, LANES)], tabv.at[:, pl.ds(0, LANES)], lsem.at[2])
    get_shift = pltpu.make_async_copy(tab.at[:, pl.ds(scol, LANES)], tabv.at[:, pl.ds(LANES, LANES)], lsem.at[3])
    for copy in (get_go, get_in, get_scale, get_shift):
        copy.start()

    barrier = pltpu.get_barrier_semaphore()

    @pl.loop(1, 8)
    def _(d):
        pl.semaphore_signal(barrier, inc=1, device_id=gpeer((m + d) % G), device_id_type=MESH)
        pl.semaphore_signal(barrier, inc=1, device_id=zpeer((z + d) % NZ), device_id_type=MESH)
        pl.semaphore_signal(barrier, inc=1, device_id=ypeer((y + d) % NY), device_id_type=MESH)

    @pl.loop(0, NX)
    def _(i):
        pl.semaphore_signal(barrier, inc=1, device_id=hpeer(i), device_id_type=MESH)

    row8 = iota((8, LANES), 0)
    lane = iota((8, LANES), 1)
    info = jnp.where(lane == 0, part[0, 0], 0)
    info = jnp.where(lane == 1, qb[0, 0, 0], info)
    info = jnp.where(lane == 2, qb[0, 0, 1], info)
    info = jnp.where(lane == 3, clip[0], info).astype(F32)
    wrow = w[...].astype(F32)
    for i in range(G):
        qi, ci = i // 2, i % 2
        taps = (1, 3) if ci == 0 else (2, 0)
        first, second = [wrow[:, k * C + qi * LANES : k * C + (qi + 1) * LANES] for k in taps]
        tsend[i] = jnp.where(row8 == 0, first, jnp.where(row8 == 1, second, info))
    tg[m] = tsend[m]

    pl.semaphore_wait(barrier, 25)

    spread(TILE, m, gpeer, lambda i: tsend.at[i], tg.at[m])
    spread(INP, x, xpeer, lambda i: inp.at[0], xg.at[m], n=NX)
    own_in = remote(inp.at[0], xg.at[m], INP, 0, 0, sibling)
    own_in.start()
    pending.append(own_in.wait_send)

    turn = (c * ((y + 1) // NY) + (1 - c) * (3 * ((NY - y) // NY))) % NX

    def halo_copy(i):
        src = inp.at[0, pl.ds(pl.multiple_of(c * 112, 16), 16), :]
        return remote(src, hx.at[(x + turn) % NX], HALO, i, (x + turn) % NX, hpeer(i))

    @pl.loop(0, NX)
    def _(i):
        halo_copy(i).start()

    def halo_sent():
        @pl.loop(0, NX)
        def _(i):
            halo_copy(i).wait_send()

    pending.append(halo_sent)

    get_go.wait()
    ri, rj = iota((256, 256), 0), iota((256, 256), 1)
    pick = jnp.where(ri < ROWS, 2 * ri, 2 * (ri - ROWS) + 1)
    gde = dot(jnp.where(rj == pick, 1.0, 0.0).astype(BF16), gov[...]).astype(BF16)
    for i in range(G):
        qi, ci = i // 2, i % 2
        gsend[i] = gde[ci * ROWS : (ci + 1) * ROWS, qi * LANES : (qi + 1) * LANES]
    gg[m] = gsend[m]
    spread(GOUT, m, gpeer, lambda i: gsend.at[i], gg.at[m])

    collect(TILE, m, gpeer, lambda i: tg.at[i])
    rows_a = jnp.zeros((8, LANES), F32)
    rows_b = rows_a
    ids = rows_a
    for i in range(G):
        tile = tg[i]
        rows_a = jnp.where(row8 == i, tile[0:1], rows_a)
        rows_b = jnp.where(row8 == i, tile[1:2], rows_b)
        ids = jnp.where(row8 == i, tile[2:3], ids)
    idz[z] = ids
    wy[y, z] = jnp.concatenate([rows_a, rows_b], 0).astype(BF16)
    spread(IDZ, z, zpeer, lambda i: idz.at[z], idz.at[z])
    spread(WZ, z, zpeer, lambda i: wy.at[y, z], wy.at[y, z])

    @pl.loop(0, 8)
    def _(b):
        row = b * LANES + iota((LANES, LANES), 0)
        tap, chan = row // C, row % C
        place = (chan // 2) % 8 * 128 + chan // 64 * 16 + tap * 8 + chan // 16 % 4 * 2 + chan % 2
        off = place - iota((LANES, LANES), 1)
        for k in range(8):
            p01[pl.ds(pl.multiple_of(b * LANES, LANES), LANES), k * LANES : (k + 1) * LANES] = jnp.where(
                off == k * LANES, 1.0, 0.0
            ).astype(BF16)

    collect(WZ, z, zpeer, lambda i: wy.at[y, i])
    spread(WY, y, ypeer, lambda i: wy.at[y], wy.at[y])

    collect(IDZ, z, zpeer, lambda i: idz.at[i])
    base = (z * C).astype(F32)
    lane512 = iota((8, C), 1).astype(F32)
    packed = jnp.zeros((8, LANES), F32)
    asked = []
    for i in range(NZ):
        tile = idz[i]
        part_id, clip_id = tile[:, 0:1], tile[:, 3:4]
        asked.append(jnp.where(part_id - base == lane512, 1.0, 0.0))
        asked.append(jnp.where(clip_id - base == lane512, 1.0, 0.0))
        packed = jnp.where(lane == i, part_id, jnp.where(lane == 8 + i, clip_id, packed))
    idy[y] = packed
    spread(IDY, y, ypeer, lambda i: idy.at[y], idy.at[y])
    get_scale.wait()
    get_shift.wait()
    served = dot(jnp.concatenate(asked, 0).astype(BF16), tabv[...]).astype(BF16)
    for i in range(NZ):
        frs[i] = served[16 * i : 16 * (i + 1)]
    frr[z] = frs[z]
    spread(FILM, z, zpeer, lambda i: frs.at[i], frr.at[z])

    def hand_on(d):
        i = (x - d + NX) % NX
        return remote(xg.at[2 * i + c], xg.at[2 * i + c], INP, 4 + d, 4 + d, sibling)

    @pl.loop(1, NX)
    def _(d):
        i = (x - d + NX) % NX
        remote(xg.at[2 * i + c], xg.at[2 * i + c], INP, d, d, xpeer(i)).wait_recv()
        hand_on(d).start()

    def handed_on():
        @pl.loop(1, NX)
        def _(d):
            hand_on(d).wait_send()

    pending.append(handed_on)

    get_in.wait()
    remote(xg.at[2 * x + 1 - c], xg.at[2 * x + 1 - c], INP, 0, 0, sibling).wait_recv()

    @pl.loop(1, NX)
    def _(d):
        i = (x - d + NX) % NX
        remote(xg.at[2 * i + 1 - c], xg.at[2 * i + 1 - c], INP, 4 + d, 4 + d, sibling).wait_recv()

    @pl.loop(0, NX)
    def _(i):
        remote(hx.at[i], hx.at[i], HALO, i, i, hpeer(i)).wait_recv()

    shift = jnp.where(rj - ri == side, 1.0, 0.0).astype(BF16)
    rowp = iota((256, C), 0)
    for i in range(NX):
        pair = xg[2 * i : 2 * i + 2].reshape(256, C)
        block = hx[i].astype(F32)
        outer = jnp.where(c == 0, block[15:16], block[0:1])
        inside = i * 16 + y * 2 + c != c * 63
        outer = jnp.where(inside, outer, 0.0)
        moved = jnp.where(rowp == c * 255, outer, dot(shift, pair))
        xs[256 * i : 256 * (i + 1)] = moved.astype(BF16)

    collect(IDY, y, ypeer, lambda i: idy.at[i])
    for i in range(NZ):
        for k in range(NY):
            match = jnp.where(idy[k][:, i : i + 1] - base == lane512, 1.0, 0.0)
            if k % 2 == 0:
                even = match
            else:
                pickt[80 * i + 8 * (k - 1) : 80 * i + 8 * (k + 1)] = jnp.concatenate([even, match], 0).astype(BF16)
        match = jnp.where(idy[0][:, 8 + i : 9 + i] - base == lane512, 1.0, 0.0)
        pickt[80 * i + 64 : 80 * i + 80] = jnp.concatenate([match, match], 0).astype(BF16)

    collect(FILM, z, zpeer, lambda i: frr.at[i])
    film = frr[0].astype(F32)
    for i in range(1, NZ):
        film = film + frr[i].astype(F32)
    flm[...] = film
    collect(GOUT, m, gpeer, lambda i: gg.at[i])
    collect(WY, y, ypeer, lambda i: wy.at[i])

    wcat[...] = dot(p01[...], wy[...].reshape(2 * C, LANES)).astype(BF16)
    frames = xg[...].reshape(2 * C, C)
    ub[...] = dot(frames, wcat[0:C]) + dot(xs[...], wcat[C : 2 * C])

    base_row = flm[8:9]
    frame = (2 * iota((ROWS, LANES), 0) + c).astype(F32)
    part_scale = jnp.zeros((8, LANES), F32)
    part_shift = part_scale
    base_scale = jnp.zeros((1, LANES), F32)
    base_shift = base_scale
    for i in range(G):
        u = ub[ROWS * i : ROWS * (i + 1)]
        bounds = tg[i]
        quoted = (frame >= bounds[2:3, 1:2]) & (frame < bounds[2:3, 2:3])
        scale = jnp.where(quoted, flm[i : i + 1, 0:LANES], base_row[:, 0:LANES])
        offset = jnp.where(quoted, flm[i : i + 1, LANES:], base_row[:, LANES:])
        gain = 1.0 + scale
        grad = gg[i].astype(F32) * mish_slope(u * gain + offset)
        gbuf[ROWS * i : ROWS * (i + 1)] = (grad * gain).astype(BF16)
        gu = grad * u
        part_scale = jnp.where(row8 == i, jnp.sum(jnp.where(quoted, gu, 0.0), 0, keepdims=True), part_scale)
        part_shift = jnp.where(row8 == i, jnp.sum(jnp.where(quoted, grad, 0.0), 0, keepdims=True), part_shift)
        base_scale = base_scale + jnp.sum(jnp.where(quoted, 0.0, gu), 0, keepdims=True)
        base_shift = base_shift + jnp.sum(jnp.where(quoted, 0.0, grad), 0, keepdims=True)
    fscale = 1.0 / 16.0
    segs[0] = jnp.concatenate([part_scale, jnp.where(row8 == 0, base_scale, 0.0)], 0) * fscale
    segs[1] = jnp.concatenate([part_shift, jnp.where(row8 == 0, base_shift, 0.0)], 0) * fscale
    pair_copy = remote(segs.at[1 - c], c1r, PAIR, 0, 0, sibling)
    pair_copy.start()

    gall = gbuf[...]
    gw0 = dot_tn(gall, frames).astype(BF16)
    gw1 = dot_tn(gall, xs[...]).astype(BF16)
    gwp = (dot(gw0, p01[0:C]) + dot(gw1, p01[C : 2 * C])).astype(BF16)
    for i in range(NY):
        gws[i] = gwp[:, LANES * i : LANES * (i + 1)]
    gwr[y] = gws[y]
    spread(GWY, y, ypeer, lambda i: gws.at[i], gwr.at[y])

    back = jnp.where(ri - rj == side, 1.0, 0.0).astype(BF16)
    edges = jnp.zeros((8, LANES), F32)
    for i in range(NX):
        pair = gbuf[256 * i : 256 * (i + 1)]
        moved = dot(back, pair).astype(BF16)
        grads = dot_nt(pair, wcat[0:C]) + dot_nt(moved, wcat[C : 2 * C])
        pb[2 * i] = grads[0:ROWS]
        pb[2 * i + 1] = grads[ROWS:]
        gis[i] = pb[2 * i + 1 - c].astype(BF16)
        remote(gis.at[i], gir.at[i], GID, i, i, sibling).start()
        outer = jnp.where(c == 0, pair[0:16].astype(F32)[0:1], pair[240:256].astype(F32)[15:16])
        edges = jnp.where(row8 == i, outer, edges)
    edge_rows = dot_nt(edges.astype(BF16), wcat[C : 2 * C])

    def edge_copy(i):
        return remote(esend.at[i], ed.at[x], EDGE, i, x, hpeer((i + turn) % NX))

    for i in range(NX):
        esend[i] = jnp.broadcast_to(edge_rows[i : i + 1], (8, C))

    @pl.loop(0, NX)
    def _(i):
        edge_copy(i).start()

    pair_copy.wait_recv()
    yr[y] = segs[c] + c1r[...]
    spread(ROWY, y, ypeer, lambda i: yr.at[y], yr.at[y])

    for i in range(NX):
        remote(gis.at[i], gir.at[i], GID, i, i, sibling).wait_recv()
        total = pb[2 * i + c] + gir[i].astype(F32)
        pb[2 * i + c] = total
        gi2[i] = total.astype(BF16)
    spread(GIX, x, xpeer, lambda i: gi2.at[i], gix.at[x], n=NX)

    collect(ROWY, y, ypeer, lambda i: yr.at[i])
    sums = yr[0, 8:16]
    for i in range(1, NY):
        sums = sums + yr[i, 8:16]
    pieces = [yr[i, 0:8] for i in range(NY)] + [sums, jnp.zeros((8, LANES), F32)]
    zr[z] = jnp.concatenate(pieces, 0).astype(BF16)
    spread(ROWZ, z, zpeer, lambda i: zr.at[z], zr.at[z])

    collect(GWY, y, ypeer, lambda i: gwr.at[i])
    gsum = gwr[0].astype(F32)
    for i in range(1, NY):
        gsum = gsum + gwr[i].astype(F32)
    turned = gsum.T
    for i in range(NZ):
        gz[i] = turned[16 * i : 16 * (i + 1)]
    gzr[z] = gz[z]
    spread(GWZ, z, zpeer, lambda i: gz.at[i], gzr.at[z])

    ocol = pl.multiple_of(c * C + x * LANES, LANES)
    collect(ROWZ, z, zpeer, lambda i: zr.at[i])
    o_gt[:, pl.ds(ocol, LANES)] = dot_tn(pickt[...], zr[...].reshape(640, LANES)).astype(BF16)
    mine = o_gt.at[:, pl.ds(ocol, LANES)]
    spread(TAB, x, xpeer, lambda i: mine, mine, n=NX)
    own_tab = remote(mine, mine, TAB, 0, 0, sibling)
    own_tab.start()
    pending.append(own_tab.wait_send)

    collect(GWZ, z, zpeer, lambda i: gzr.at[i])
    gsum = gzr[0]
    for i in range(1, NZ):
        gsum = gsum + gzr[i]
    gsum = gsum * (1.0 / 256.0)
    for i in range(G):
        gxs[i] = jnp.where(row8 == 0, gsum[i : i + 1], gsum[8 + i : 9 + i])
    gxr[m] = gxs[m]
    spread(GWX, m, gpeer, lambda i: gxs.at[i], gxr.at[m])

    collect(GIX, x, xpeer, lambda i: gix.at[i], n=NX)

    @pl.loop(0, NX)
    def _(i):
        remote(ed.at[i], ed.at[i], EDGE, i, i, hpeer(i)).wait_recv()

    gix[x] = jnp.zeros((ROWS, C), BF16)
    total = pb[2 * x + c]
    edge = ed[0, 0:1]
    for i in range(NX):
        total = total + gix[i].astype(F32)
        if i:
            edge = edge + ed[i, 0:1]
    edge = jnp.where(s != c * 63, edge, 0.0)
    total = total + jnp.where(iota((ROWS, C), 0) == c * 127, edge, 0.0)
    o_gi[0] = total.astype(BF16)

    collect(GWX, m, gpeer, lambda i: gxr.at[i])
    for i in range(G):
        qi, ci = i // 2, i % 2
        taps = (1, 3) if ci == 0 else (2, 0)
        for t, k in enumerate(taps):
            o_gw[:, k * C + qi * LANES : k * C + (qi + 1) * LANES] = gxr[i, t : t + 1]

    def column(i, cc):
        return o_gt.at[:, pl.ds(pl.multiple_of(cc * C + i * LANES, LANES), LANES)]

    def pass_on(d):
        i = (x - d + NX) % NX
        return remote(column(i, c), column(i, c), TAB, 4 + d, 4 + d, sibling)

    @pl.loop(1, NX)
    def _(d):
        i = (x - d + NX) % NX
        remote(column(i, c), column(i, c), TAB, d, d, xpeer(i)).wait_recv()
        pass_on(d).start()

    remote(column(x, 1 - c), column(x, 1 - c), TAB, 0, 0, sibling).wait_recv()

    @pl.loop(1, NX)
    def _(d):
        i = (x - d + NX) % NX
        remote(column(i, 1 - c), column(i, 1 - c), TAB, 4 + d, 4 + d, sibling).wait_recv()

    pair_copy.wait_send()
    for i in range(NX):
        remote(gis.at[i], gir.at[i], GID, i, i, sibling).wait_send()

    @pl.loop(0, NX)
    def _(i):
        edge_copy(i).wait_send()

    @pl.loop(1, NX)
    def _(d):
        pass_on(d).wait_send()

    for finish in pending:
        finish()


def body(inputs, weight, table, grad_out, clip_speaker, part_speaker, quote_bounds):
    vmem = pl.BlockSpec(memory_space=pltpu.VMEM)
    smem = pl.BlockSpec(memory_space=pltpu.SMEM)
    hbm = pl.BlockSpec(memory_space=pl.ANY)
    V = pltpu.VMEM
    return pl.pallas_call(
        kernel,
        out_shape=(
            jax.ShapeDtypeStruct(inputs.shape, BF16),
            jax.ShapeDtypeStruct(weight.shape, F32),
            jax.ShapeDtypeStruct(table.shape, BF16),
        ),
        in_specs=[hbm, vmem, hbm, hbm, smem, smem, smem],
        out_specs=(vmem, vmem, vmem),
        scratch_shapes=[
            V((G, 8, LANES), F32),
            V((G, 8, LANES), F32),
            V((NZ, 8, LANES), F32),
            V((NY, 8, LANES), F32),
            V((NY, NZ, 16, LANES), BF16),
            V((C, 2 * LANES), BF16),
            V((NZ, 16, 2 * LANES), BF16),
            V((NZ, 16, 2 * LANES), BF16),
            V((16, 2 * LANES), F32),
            V((G, ROWS, C), BF16),
            V((NX, 16, C), BF16),
            V((G * ROWS, C), BF16),
            V((2 * ROWS, C), BF16),
            V((G, ROWS, LANES), BF16),
            V((G, ROWS, LANES), BF16),
            V((2 * C, 2 * C), BF16),
            V((2 * C, LANES), BF16),
            V((640, C), BF16),
            V((G * ROWS, LANES), F32),
            V((G * ROWS, LANES), BF16),
            V((2, 16, LANES), F32),
            V((16, LANES), F32),
            V((NY, 16, LANES), F32),
            V((NZ, 80, LANES), BF16),
            V((NY, LANES, LANES), BF16),
            V((NY, LANES, LANES), BF16),
            V((NZ, 16, LANES), F32),
            V((NZ, 16, LANES), F32),
            V((G, 8, LANES), F32),
            V((G, 8, LANES), F32),
            V((G, ROWS, C), F32),
            V((NX, ROWS, C), BF16),
            V((NX, ROWS, C), BF16),
            V((NX, ROWS, C), BF16),
            V((NX, ROWS, C), BF16),
            V((NX, 8, C), F32),
            V((NX, 8, C), F32),
            pltpu.SemaphoreType.DMA((CHANNELS, 8)),
            pltpu.SemaphoreType.DMA((CHANNELS, 8)),
            pltpu.SemaphoreType.DMA((4,)),
        ],
        compiler_params=pltpu.CompilerParams(
            collective_id=0, has_side_effects=True, vmem_limit_bytes=48 * 1024 * 1024
        ),
        cost_estimate=pl.CostEstimate(flops=2_000_000_000, bytes_accessed=8_000_000, transcendentals=131072),
    )(inputs, weight, table, grad_out, clip_speaker, part_speaker, quote_bounds)


def solution(mesh):
    placed = (
        P("dp", "seq", None),
        P(("dp", "seq"), None),
        P("dp", None),
        P("dp", "seq", None),
        P("dp"),
        P("dp", "seq"),
        P("dp", "seq", None),
    )
    return jax.shard_map(
        body,
        mesh=mesh,
        in_specs=placed,
        out_specs=(P("dp", "seq", None), P(("dp", "seq"), None), P("dp", None)),
        check_vma=False,
    )
```

time: 462 us -> 77.6 us (0.17)
  blocking collectives: 301 us -> 0 us
  waiting for transfers between devices: 94.9 us -> 0 us
  Pallas kernels: 0 us -> 69.4 us
  starting transfers between devices: 19.7 us -> 0 us
  between operations: 16.2 us -> 1.97 us
  matrix products: 12.5 us -> 0 us
  other arithmetic: 7.14 us -> 0 us
    psum x1 -> x0, blocking collectives: 269 us -> none  [body(): table_sum = lax.psum(owned_rows(gathered, speakers, own_count), 'seq')]
    all_gather x1 -> x0, waiting for transfers between devices: 90.5 us -> none  [body(): full_weight = lax.all_gather(weight, ('dp', 'seq'), axis=0, tiled=True)]
    pallas_call x0 -> x1, Pallas kernels: none -> 69.4 us  [body(): pl.pallas_call(kernel, out_shape=(jax.ShapeDtypeStruct(inputs.shape, BF16...]
    all_gather x1 -> x0, blocking collectives: 19.2 us -> none  [body(): lax.all_gather(segment, 'dp', axis=0, tiled=True)]
    ppermute x4 -> x0, starting transfers between devices: 16.3 us -> none  [the longest x2 10.9 us: padded(): after = lax.ppermute(leading, axis, down)]
    dot_general x6 -> x0, matrix products: 12.5 us -> none  [the longest x1 4.2 us: body(): lax.dot_general(taps_grad, full_weight, (((1,), (1,)), ((), ())), preferr...]
    unnamed x1 -> x0, blocking collectives: 12.1 us -> none
  transfers between devices with their start and end apart: 7 -> 0, of which waited for: 3 -> 0; matrix products, arithmetic and copies ran while one was open for 3% -> 0% of each run, Pallas kernels for 0% -> 0%
where the time goes in v1:
time: 77.6 us; the launch traced here: 77.3 us
  Pallas kernels  69.4 us (89%)
  local copies, waits for them, and re-layouts  6 us (8%)
  between operations  1.97 us (3%)
    pallas_call x1, Pallas kernels, body(): pl.pallas_call(kernel, out_shape=(jax.ShapeDtypeStruct(inputs.shape, BF16...  69.4 us
    unnamed x13, local copies, waits for them, and re-layouts  6 us

profile of v1, /device:TPU:1, one launch (start us, length us, event | category | flops | bytes accessed | tf_op | source)
XLA Modules:
  0.0 77.3 jit_solution(9953886860296297)
XLA Ops:
  1.3 0.0 copy-start.4
  1.9 0.0 copy-done.4
  2.0 0.0 copy-start
  2.0 1.2 %copy-done = bf16[512,1024]{1,0:T(8,128)(2,1)S(1)} copy-done((bf16[512,1024]{1,0:T(8,128)(2,1)S(1)}, bf16[512,1024]{1,0:T(8,128)(2,1)}, u32[]{:S(2)}) %copy-start) | copy-done | bytes 1048600
  3.2 0.0 copy-start.1
  3.2 0.9 %copy-done.1 = bf16[1,256,512]{2,1,0:T(8,128)(2,1)S(1)} copy-done((bf16[1,256,512]{2,1,0:T(8,128)(2,1)S(1)}, bf16[1,256,512]{2,1,0:T(8,128)(2,1)}, u32[]{:S(2)}) %copy-start.1) | copy-done | bytes 262168
  4.1 0.0 copy-start.2
  4.1 0.9 %copy-done.2 = bf16[1,128,512]{2,1,0:T(8,128)(2,1)S(1)} copy-done((bf16[1,128,512]{2,1,0:T(8,128)(2,1)S(1)}, bf16[1,128,512]{2,1,0:T(8,128)(2,1)}, u32[]{:S(2)}) %copy-start.2) | copy-done | bytes 131096
  5.0 0.0 copy-start.3
  5.0 0.7 copy-done.3
  5.7 69.4 %shard_map.94 = (bf16[1,128,512]{2,1,0:T(8,128)(2,1)S(1)}, f32[1,2048]{1,0:T(1,128)S(1)}, bf16[512,1024]{1,0:T(8,128)(2,1)S(1)}) custom-call(bf16[1,128,512]{2,1,0:T(8,128)(2,1)S(1)} %copy-done.2, bf16[1,2048]{1,0:T(2,128)(2,1)S(1)} %copy-done.3, bf16[512,1024]{1,0:T(8,128)(2,1)S(1)} %copy-done, bf16[1,256,512]{2,1,0:T(8,128)(2,1)S(1)} %copy-done.1, ...), custom_call_target="tpu_custom_call" | custom-call | flops 2000000000 | bytes 8000000 | tf_op jit(solution)/shard_map/pallas_call | solution.py:467
  75.1 0.7 copy.15
  75.8 0.6 copy.16
  76.4 1.0 %copy.17 = bf16[512,1024]{1,0:T(8,128)(2,1)} copy(bf16[512,1024]{1,0:T(8,128)(2,1)S(1)} %get-tuple-element.8) | data formatting | bytes 2097152
Async XLA Ops:
  1.3 0.7 copy-start.4
  2.0 1.2 %copy-start = (bf16[512,1024]{1,0:T(8,128)(2,1)S(1)}, bf16[512,1024]{1,0:T(8,128)(2,1)}, u32[]{:S(2)}) copy-start(bf16[512,1024]{1,0:T(8,128)(2,1)} %tab.1) | copy-start | bytes 3145732
  3.2 0.9 %copy-start.1 = (bf16[1,256,512]{2,1,0:T(8,128)(2,1)S(1)}, bf16[1,256,512]{2,1,0:T(8,128)(2,1)}, u32[]{:S(2)}) copy-start(bf16[1,256,512]{2,1,0:T(8,128)(2,1)} %go.1) | copy-start | bytes 786436
  4.1 0.9 %copy-start.2 = (bf16[1,128,512]{2,1,0:T(8,128)(2,1)S(1)}, bf16[1,128,512]{2,1,0:T(8,128)(2,1)}, u32[]{:S(2)}) copy-start(bf16[1,128,512]{2,1,0:T(8,128)(2,1)} %inp.1) | copy-start | bytes 393220
  5.0 0.7 copy-start.3

commit v2 on v1

v2 whole, which is shorter than its diff:
```python
import jax
import jax.numpy as jnp
from jax import lax
from jax.experimental import pallas as pl
from jax.experimental.pallas import tpu as pltpu
from jax.sharding import PartitionSpec as P

MESH = pl.DeviceIdType.MESH
F32 = jnp.float32
BF16 = jnp.bfloat16

NX, NY, NZ = 4, 8, 8
G = 8
C = 512
ROWS = 128
LANES = 128

(TILE, IDZ, WZ, WY, FILM, IDY, GOUT, ROWY, ROWZ, GWY, GWZ, GWX, HALO, PAIR, GID, GIX, EDGE) = range(17)
INP, TAB = 17, 22
CHANNELS = 27


def iota(shape, dim):
    return lax.broadcasted_iota(jnp.int32, shape, dim)


def dot(a, b):
    return jnp.dot(a, b, preferred_element_type=F32)


def dot_nt(a, b):
    return lax.dot_general(a, b, (((1,), (1,)), ((), ())), preferred_element_type=F32)


def dot_tn(a, b):
    return lax.dot_general(a, b, (((0,), (0,)), ((), ())), preferred_element_type=F32)


def mish_slope(pre):
    t = jnp.exp(-jnp.abs(pre))
    positive = pre >= 0.0
    num = jnp.where(positive, 1.0 + 2.0 * t, t * (t + 2.0))
    rest = jnp.where(positive, 2.0 * t * t, 2.0)
    inv = 1.0 / (num + rest)
    tangent = num * inv
    gate = jnp.where(positive, 1.0, t) / (1.0 + t)
    return tangent + pre * gate * (rest * (2.0 * num + rest) * inv * inv)


def kernel(
    inp, whbm, tab, go, clip, part, qb, o_gi, o_gw, o_gt, w,
    tsend, tg, idz, idy, wy, tabv, frs, frr, flm, xg, hx, xx, gov, gsend, gg, p01, wcat, pickt,
    gbuf, segs, c1r, yr, zr, gws, gwr, gz, gzr, gxs, gxr, pb, gis, gir, gi2, gix, esend, ed,
    ssem, rsem, lsem,
):
    z = lax.axis_index("dp")
    s = lax.axis_index("seq")
    x = s // 16
    y = (s // 2) % NY
    c = s % 2
    m = 2 * x + c
    side = 2 * c - 1

    def at(zz, xx, yy, cc):
        return (zz, xx * 16 + yy * 2 + cc)

    def gpeer(i):
        return at(z, i // 2, y, i % 2)

    def ypeer(i):
        return at(z, x, i, c)

    def zpeer(i):
        return at(i, x, y, c)

    def xpeer(i):
        return at(z, i, y, c)

    sibling = at(z, x, y, 1 - c)

    def hpeer(i):
        return at(z, i, (y + side + NY) % NY, 1 - c)

    def remote(src, dst, send, recv, dev):
        return pltpu.make_async_remote_copy(
            src_ref=src, dst_ref=dst, send_sem=ssem.at[send], recv_sem=rsem.at[recv],
            device_id=dev, device_id_type=MESH,
        )

    pending = []
    waiting = {}

    def watch(chan, ref):
        whole = remote(ref, ref, chan, chan, sibling)
        pending.append(whole.wait_send)
        waiting[chan] = whole.wait_recv

    def spread(chan, me, peer, src, slot, whole, n=8):
        @pl.loop(1, n)
        def _(d):
            i = (me + d) % n
            remote(src(i), slot(me), chan, chan, peer(i)).start()

        watch(chan, whole)

    def collect(chan):
        waiting.pop(chan)()

    def x_spread(base, src, slot, slots):
        @pl.loop(1, NX)
        def _(d):
            remote(src, slot(x, c), base, base + d, xpeer((x + d) % NX)).start()

        remote(src, slot(x, c), base, base, sibling).start()
        pending.append(remote(slots(4), slots(4), base, base, sibling).wait_send)
        waiting[base] = remote(slot(x, 1 - c), slot(x, 1 - c), base, base, sibling).wait_recv
        for d in range(1, NX):
            mine = slot((x - d + NX) % NX, c)
            waiting[base + d] = remote(mine, mine, base, base + d, sibling).wait_recv

    def x_hand_on(base, slot, slots):
        for d in range(1, NX):
            collect(base + d)
            mine = slot((x - d + NX) % NX, c)
            remote(mine, mine, base + 4, base + 4, sibling).start()

        watch(base + 4, slots(3))

    def column(i, cc):
        return o_gt.at[:, pl.ds(pl.multiple_of(cc * C + i * LANES, LANES), LANES)]

    def columns(n):
        return o_gt.at[:, pl.ds(0, n * LANES)]

    barrier = pltpu.get_barrier_semaphore()

    @pl.loop(1, 8)
    def _(d):
        pl.semaphore_signal(barrier, inc=1, device_id=gpeer((m + d) % G), device_id_type=MESH)
        pl.semaphore_signal(barrier, inc=1, device_id=zpeer((z + d) % NZ), device_id_type=MESH)
        pl.semaphore_signal(barrier, inc=1, device_id=ypeer((y + d) % NY), device_id_type=MESH)

    @pl.loop(0, NX)
    def _(i):
        pl.semaphore_signal(barrier, inc=1, device_id=hpeer(i), device_id_type=MESH)

    xcol = pl.multiple_of(x * LANES, LANES)
    scol = pl.multiple_of(C + x * LANES, LANES)
    get_go = pltpu.make_async_copy(go.at[0], gov, lsem.at[0])
    get_in = pltpu.make_async_copy(inp.at[0], xg.at[m], lsem.at[1])
    get_scale = pltpu.make_async_copy(tab.at[:, pl.ds(xcol, LANES)], tabv.at[:, pl.ds(0, LANES)], lsem.at[2])
    get_shift = pltpu.make_async_copy(tab.at[:, pl.ds(scol, LANES)], tabv.at[:, pl.ds(LANES, LANES)], lsem.at[3])
    get_w = pltpu.make_async_copy(whbm, w, lsem.at[4])
    for copy in (get_w, get_go, get_in, get_scale, get_shift):
        copy.start()

    row8 = iota((8, LANES), 0)
    lane = iota((8, LANES), 1)
    info = jnp.where(lane == 0, part[0, 0], 0)
    info = jnp.where(lane == 1, qb[0, 0, 0], info)
    info = jnp.where(lane == 2, qb[0, 0, 1], info)
    info = jnp.where(lane == 3, clip[0], info).astype(F32)
    get_w.wait()
    wrow = w[...].astype(F32)
    for i in range(G):
        qi, ci = i // 2, i % 2
        taps = (1, 3) if ci == 0 else (2, 0)
        first, second = [wrow[:, k * C + qi * LANES : k * C + (qi + 1) * LANES] for k in taps]
        tsend[i] = jnp.where(row8 == 0, first, jnp.where(row8 == 1, second, info))
    tg[m] = tsend[m]

    pl.semaphore_wait(barrier, 25)

    spread(TILE, m, gpeer, lambda i: tsend.at[i], lambda i: tg.at[i], tg.at[pl.ds(0, 7)])

    def frame_slot(i, cc):
        return xg.at[2 * i + cc]

    def frame_slots(n):
        return xg.at[pl.ds(0, n)]

    x_spread(INP, inp.at[0], frame_slot, frame_slots)
    turn = (c * ((y + 1) // NY) + (1 - c) * (3 * ((NY - y) // NY))) % NX

    @pl.loop(0, NX)
    def _(i):
        src = inp.at[0, pl.ds(pl.multiple_of(c * 112, 16), 16), :]
        remote(src, hx.at[(x + turn) % NX], HALO, HALO, hpeer(i)).start()

    watch(HALO, hx)

    get_go.wait()
    ri, rj = iota((256, 256), 0), iota((256, 256), 1)
    pick = jnp.where(ri < ROWS, 2 * ri, 2 * (ri - ROWS) + 1)
    gde = dot(jnp.where(rj == pick, 1.0, 0.0).astype(BF16), gov[...]).astype(BF16)
    for i in range(G):
        qi, ci = i // 2, i % 2
        gsend[i] = gde[ci * ROWS : (ci + 1) * ROWS, qi * LANES : (qi + 1) * LANES]
    gg[m] = gsend[m]
    spread(GOUT, m, gpeer, lambda i: gsend.at[i], lambda i: gg.at[i], gg.at[pl.ds(0, 7)])

    collect(TILE)
    rows_a = jnp.zeros((8, LANES), F32)
    rows_b = rows_a
    ids = rows_a
    for i in range(G):
        tile = tg[i]
        rows_a = jnp.where(row8 == i, tile[0:1], rows_a)
        rows_b = jnp.where(row8 == i, tile[1:2], rows_b)
        ids = jnp.where(row8 == i, tile[2:3], ids)
    idz[z] = ids
    wy[y, z] = jnp.concatenate([rows_a, rows_b], 0).astype(BF16)
    spread(IDZ, z, zpeer, lambda i: idz.at[z], lambda i: idz.at[i], idz.at[pl.ds(0, 7)])
    spread(WZ, z, zpeer, lambda i: wy.at[y, z], lambda i: wy.at[y, i], wy.at[y, pl.ds(0, 7)])

    @pl.loop(0, 8)
    def _(b):
        row = b * LANES + iota((LANES, LANES), 0)
        tap, chan = row // C, row % C
        place = (chan // 2) % 8 * 128 + chan // 64 * 16 + tap * 8 + chan // 16 % 4 * 2 + chan % 2
        off = place - iota((LANES, LANES), 1)
        for k in range(8):
            p01[pl.ds(pl.multiple_of(b * LANES, LANES), LANES), k * LANES : (k + 1) * LANES] = jnp.where(
                off == k * LANES, 1.0, 0.0
            ).astype(BF16)

    collect(WZ)
    spread(WY, y, ypeer, lambda i: wy.at[y], lambda i: wy.at[i], wy.at[pl.ds(0, 7)])

    collect(IDZ)
    base = (z * C).astype(F32)
    lane512 = iota((8, C), 1).astype(F32)
    packed = jnp.zeros((8, LANES), F32)
    asked = []
    for i in range(NZ):
        tile = idz[i]
        part_id, clip_id = tile[:, 0:1], tile[:, 3:4]
        asked.append(jnp.where(part_id - base == lane512, 1.0, 0.0))
        asked.append(jnp.where(clip_id - base == lane512, 1.0, 0.0))
        packed = jnp.where(lane == i, part_id, jnp.where(lane == 8 + i, clip_id, packed))
    idy[y] = packed
    spread(IDY, y, ypeer, lambda i: idy.at[y], lambda i: idy.at[i], idy.at[pl.ds(0, 7)])
    get_scale.wait()
    get_shift.wait()
    served = dot(jnp.concatenate(asked, 0).astype(BF16), tabv[...]).astype(BF16)
    for i in range(NZ):
        frs[i] = served[16 * i : 16 * (i + 1)]
    frr[z] = frs[z]
    spread(FILM, z, zpeer, lambda i: frs.at[i], lambda i: frr.at[i], frr.at[pl.ds(0, 7)])

    x_hand_on(INP, frame_slot, frame_slots)
    get_in.wait()
    collect(INP)
    collect(INP + 4)
    collect(HALO)

    shift = jnp.where(rj - ri == side, 1.0, 0.0).astype(BF16)
    rowp = iota((256, C), 0)
    for i in range(NX):
        pair = xg[2 * i : 2 * i + 2].reshape(256, C)
        block = hx[i].astype(F32)
        outer = jnp.where(c == 0, block[15:16], block[0:1])
        inside = i * 16 + y * 2 + c != c * 63
        outer = jnp.where(inside, outer, 0.0)
        moved = jnp.where(rowp == c * 255, outer, dot(shift, pair))
        xx[256 * i : 256 * (i + 1)] = (dot(pair, p01[0:C]) + dot(moved.astype(BF16), p01[C : 2 * C])).astype(BF16)

    collect(FILM)
    film = frr[0].astype(F32)
    for i in range(1, NZ):
        film = film + frr[i].astype(F32)
    flm[...] = film
    collect(GOUT)
    collect(WY)

    arrived = wy[...].reshape(2 * C, LANES)
    base_row = flm[8:9]
    frame = (2 * iota((ROWS, LANES), 0) + c).astype(F32)
    part_scale = jnp.zeros((8, LANES), F32)
    part_shift = part_scale
    base_scale = jnp.zeros((1, LANES), F32)
    base_shift = base_scale
    for i in range(G):
        if i % 2 == 0:
            u_pair = dot(xx[ROWS * i : ROWS * (i + 2)], arrived)
        u = u_pair[ROWS * (i % 2) : ROWS * (i % 2 + 1)]
        bounds = tg[i]
        quoted = (frame >= bounds[2:3, 1:2]) & (frame < bounds[2:3, 2:3])
        scale = jnp.where(quoted, flm[i : i + 1, 0:LANES], base_row[:, 0:LANES])
        offset = jnp.where(quoted, flm[i : i + 1, LANES:], base_row[:, LANES:])
        gain = 1.0 + scale
        grad = gg[i].astype(F32) * mish_slope(u * gain + offset)
        gbuf[ROWS * i : ROWS * (i + 1)] = (grad * gain).astype(BF16)
        gu = grad * u
        part_scale = jnp.where(row8 == i, jnp.sum(jnp.where(quoted, gu, 0.0), 0, keepdims=True), part_scale)
        part_shift = jnp.where(row8 == i, jnp.sum(jnp.where(quoted, grad, 0.0), 0, keepdims=True), part_shift)
        base_scale = base_scale + jnp.sum(jnp.where(quoted, 0.0, gu), 0, keepdims=True)
        base_shift = base_shift + jnp.sum(jnp.where(quoted, 0.0, grad), 0, keepdims=True)
    fscale = 1.0 / 16.0
    segs[0] = jnp.concatenate([part_scale, jnp.where(row8 == 0, base_scale, 0.0)], 0) * fscale
    segs[1] = jnp.concatenate([part_shift, jnp.where(row8 == 0, base_shift, 0.0)], 0) * fscale
    remote(segs.at[1 - c], c1r, PAIR, PAIR, sibling).start()
    watch(PAIR, c1r)

    gwp = dot_tn(gbuf[...], xx[...]).astype(BF16)
    for i in range(NY):
        gws[i] = gwp[:, LANES * i : LANES * (i + 1)]

    collect(PAIR)
    yr[y] = segs[c] + c1r[...]
    spread(ROWY, y, ypeer, lambda i: yr.at[y], lambda i: yr.at[i], yr.at[pl.ds(0, 7)])
    gwr[y] = gws[y]
    spread(GWY, y, ypeer, lambda i: gws.at[i], lambda i: gwr.at[i], gwr.at[pl.ds(0, 7)])

    wcat[...] = dot(p01[...], arrived).astype(BF16)
    back = jnp.where(ri - rj == side, 1.0, 0.0).astype(BF16)
    edges = jnp.zeros((8, LANES), F32)
    for i in range(NX):
        pair = gbuf[256 * i : 256 * (i + 1)]
        moved = dot(back, pair).astype(BF16)
        grads = dot_nt(pair, wcat[0:C]) + dot_nt(moved, wcat[C : 2 * C])
        pb[2 * i] = grads[0:ROWS]
        pb[2 * i + 1] = grads[ROWS:]
        gis[i] = pb[2 * i + 1 - c].astype(BF16)
        remote(gis.at[i], gir.at[i], GID, GID, sibling).start()
        outer = jnp.where(c == 0, pair[0:16].astype(F32)[0:1], pair[240:256].astype(F32)[15:16])
        edges = jnp.where(row8 == i, outer, edges)
    watch(GID, gir)
    edge_rows = dot_nt(edges.astype(BF16), wcat[C : 2 * C])

    for i in range(NX):
        esend[i] = jnp.broadcast_to(edge_rows[i : i + 1], (8, C))

    @pl.loop(0, NX)
    def _(i):
        remote(esend.at[i], ed.at[x], EDGE, EDGE, hpeer((i + turn) % NX)).start()

    watch(EDGE, ed)
    collect(IDY)
    for i in range(NZ):
        for k in range(NY):
            match = jnp.where(idy[k][:, i : i + 1] - base == lane512, 1.0, 0.0)
            if k % 2 == 0:
                even = match
            else:
                pickt[80 * i + 8 * (k - 1) : 80 * i + 8 * (k + 1)] = jnp.concatenate([even, match], 0).astype(BF16)
        match = jnp.where(idy[0][:, 8 + i : 9 + i] - base == lane512, 1.0, 0.0)
        pickt[80 * i + 64 : 80 * i + 80] = jnp.concatenate([match, match], 0).astype(BF16)

    collect(ROWY)
    sums = yr[0, 8:16]
    for i in range(1, NY):
        sums = sums + yr[i, 8:16]
    pieces = [yr[i, 0:8] for i in range(NY)] + [sums, jnp.zeros((8, LANES), F32)]
    zr[z] = jnp.concatenate(pieces, 0).astype(BF16)
    spread(ROWZ, z, zpeer, lambda i: zr.at[z], lambda i: zr.at[i], zr.at[pl.ds(0, 7)])

    collect(GID)
    for i in range(NX):
        total = pb[2 * i + c] + gir[i].astype(F32)
        pb[2 * i + c] = total
        gi2[i] = total.astype(BF16)
    spread(GIX, x, xpeer, lambda i: gi2.at[i], lambda i: gix.at[i], gix.at[pl.ds(0, 3)], n=NX)

    collect(GWY)
    gsum = gwr[0].astype(F32)
    for i in range(1, NY):
        gsum = gsum + gwr[i].astype(F32)
    turned = gsum.T
    for i in range(NZ):
        gz[i] = turned[16 * i : 16 * (i + 1)]
    gzr[z] = gz[z]
    spread(GWZ, z, zpeer, lambda i: gz.at[i], lambda i: gzr.at[i], gzr.at[pl.ds(0, 7)])

    ocol = pl.multiple_of(c * C + x * LANES, LANES)
    collect(ROWZ)
    o_gt[:, pl.ds(ocol, LANES)] = dot_tn(pickt[...], zr[...].reshape(640, LANES)).astype(BF16)
    x_spread(TAB, column(x, c), column, columns)

    collect(GWZ)
    gsum = gzr[0]
    for i in range(1, NZ):
        gsum = gsum + gzr[i]
    gsum = gsum * (1.0 / 256.0)
    for i in range(G):
        gxs[i] = jnp.where(row8 == 0, gsum[i : i + 1], gsum[8 + i : 9 + i])
    gxr[m] = gxs[m]
    spread(GWX, m, gpeer, lambda i: gxs.at[i], lambda i: gxr.at[i], gxr.at[pl.ds(0, 7)])

    collect(GIX)
    collect(EDGE)
    gix[x] = jnp.zeros((ROWS, C), BF16)
    total = pb[2 * x + c]
    edge = ed[0, 0:1]
    for i in range(NX):
        total = total + gix[i].astype(F32)
        if i:
            edge = edge + ed[i, 0:1]
    edge = jnp.where(s != c * 63, edge, 0.0)
    total = total + jnp.where(iota((ROWS, C), 0) == c * 127, edge, 0.0)
    o_gi[0] = total.astype(BF16)

    x_hand_on(TAB, column, columns)
    collect(GWX)
    for i in range(G):
        qi, ci = i // 2, i % 2
        taps = (1, 3) if ci == 0 else (2, 0)
        for t, k in enumerate(taps):
            o_gw[:, k * C + qi * LANES : k * C + (qi + 1) * LANES] = gxr[i, t : t + 1]
    collect(TAB)
    collect(TAB + 4)

    for finish in pending:
        finish()


def place(gi, gw, gt, o_gi, o_gw, o_gt, sem):
    copies = [pltpu.make_async_copy(a, b, sem.at[k]) for k, (a, b) in enumerate(((gt, o_gt), (gi, o_gi), (gw, o_gw)))]
    for copy in copies:
        copy.start()
    for copy in copies:
        copy.wait()


def body(inputs, weight, table, grad_out, clip_speaker, part_speaker, quote_bounds):
    vmem = pl.BlockSpec(memory_space=pltpu.VMEM)
    hbm = pl.BlockSpec(memory_space=pltpu.HBM)
    smem = pl.BlockSpec(memory_space=pltpu.SMEM)
    V = pltpu.VMEM
    large = [pltpu.with_memory_space_constraint(a, pltpu.HBM) for a in (inputs, weight, table, grad_out)]
    outs = pl.pallas_call(
        kernel,
        out_shape=(
            jax.ShapeDtypeStruct(inputs.shape, BF16),
            jax.ShapeDtypeStruct(weight.shape, F32),
            jax.ShapeDtypeStruct(table.shape, BF16),
        ),
        in_specs=[hbm] * 4 + [smem] * 3,
        out_specs=(vmem, vmem, vmem),
        scratch_shapes=[
            V((1, 4 * C), BF16),
            V((G, 8, LANES), F32),
            V((G, 8, LANES), F32),
            V((NZ, 8, LANES), F32),
            V((NY, 8, LANES), F32),
            V((NY, NZ, 16, LANES), BF16),
            V((C, 2 * LANES), BF16),
            V((NZ, 16, 2 * LANES), BF16),
            V((NZ, 16, 2 * LANES), BF16),
            V((16, 2 * LANES), F32),
            V((G, ROWS, C), BF16),
            V((NX, 16, C), BF16),
            V((G * ROWS, 2 * C), BF16),
            V((2 * ROWS, C), BF16),
            V((G, ROWS, LANES), BF16),
            V((G, ROWS, LANES), BF16),
            V((2 * C, 2 * C), BF16),
            V((2 * C, LANES), BF16),
            V((640, C), BF16),
            V((G * ROWS, LANES), BF16),
            V((2, 16, LANES), F32),
            V((16, LANES), F32),
            V((NY, 16, LANES), F32),
            V((NZ, 80, LANES), BF16),
            V((NY, LANES, LANES), BF16),
            V((NY, LANES, LANES), BF16),
            V((NZ, 16, LANES), F32),
            V((NZ, 16, LANES), F32),
            V((G, 8, LANES), F32),
            V((G, 8, LANES), F32),
            V((G, ROWS, C), F32),
            V((NX, ROWS, C), BF16),
            V((NX, ROWS, C), BF16),
            V((NX, ROWS, C), BF16),
            V((NX, ROWS, C), BF16),
            V((NX, 8, C), F32),
            V((NX, 8, C), F32),
            pltpu.SemaphoreType.DMA((CHANNELS,)),
            pltpu.SemaphoreType.DMA((CHANNELS,)),
            pltpu.SemaphoreType.DMA((5,)),
        ],
        compiler_params=pltpu.CompilerParams(
            collective_id=0, has_side_effects=True, vmem_limit_bytes=48 * 1024 * 1024
        ),
        cost_estimate=pl.CostEstimate(flops=2_000_000_000, bytes_accessed=8_000_000, transcendentals=131072),
    )(*large, clip_speaker, part_speaker, quote_bounds)
    return pl.pallas_call(
        place,
        out_shape=[jax.ShapeDtypeStruct(o.shape, o.dtype) for o in outs],
        in_specs=[pl.BlockSpec(memory_space=pl.ANY)] * 3,
        out_specs=[hbm] * 3,
        scratch_shapes=[pltpu.SemaphoreType.DMA((3,))],
        compiler_params=pltpu.CompilerParams(vmem_limit_bytes=4 * 1024 * 1024),
    )(*outs)


def solution(mesh):
    placed = (
        P("dp", "seq", None),
        P(("dp", "seq"), None),
        P("dp", None),
        P("dp", "seq", None),
        P("dp"),
        P("dp", "seq"),
        P("dp", "seq", None),
    )
    return jax.shard_map(
        body,
        mesh=mesh,
        in_specs=placed,
        out_specs=(P("dp", "seq", None), P(("dp", "seq"), None), P("dp", None)),
        check_vma=False,
    )
```

time: 77.6 us -> 61.7 us (0.80)
  Pallas kernels: 69.4 us -> 59.5 us
  local copies, waits for them, and re-layouts: 6 us -> 0.01 us
    pallas_call x1, Pallas kernels: 69.4 us -> 58.5 us  [body(): pl.pallas_call(kernel, out_shape=(jax.ShapeDtypeStruct(inputs.shape, BF16...]
    unnamed x13 -> x2, local copies, waits for them, and re-layouts: 6 us -> 0.01 us
    pallas_call x0 -> x1, Pallas kernels: none -> 1.03 us  [body(): pl.pallas_call(place, out_shape=[jax.ShapeDtypeStruct(o.shape, o.dtype) f...]
where the time goes in v2:
time: 61.7 us; the launch traced here: 61.5 us
  Pallas kernels  59.5 us (96%)
  between operations  1.96 us (3%)
    pallas_call x1, Pallas kernels, body(): pl.pallas_call(kernel, out_shape=(jax.ShapeDtypeStruct(inputs.shape, BF16...  58.5 us

profile of v2, /device:TPU:1, one launch (start us, length us, event | category | flops | bytes accessed | tf_op | source)
XLA Modules:
  0.0 61.5 jit_solution(17025818229939042937)
XLA Ops:
  1.3 0.0 copy-start
  1.9 0.0 copy-done
  2.0 58.5 %shard_map.94 = (bf16[1,128,512]{2,1,0:T(8,128)(2,1)S(1)}, f32[1,2048]{1,0:T(1,128)S(1)}, bf16[512,1024]{1,0:T(8,128)(2,1)S(1)}) custom-call(bf16[1,128,512]{2,1,0:T(8,128)(2,1)} %inp.1, bf16[1,2048]{1,0:T(2,128)(2,1)} %whbm.1, bf16[512,1024]{1,0:T(8,128)(2,1)} %tab.1, bf16[1,256,512]{2,1,0:T(8,128)(2,1)} %go.1, s32[1]{0:T(128)S(6)} %copy.10.clip, ...), custom_call_target="tpu_custom_call" | custom-call | flops 2000000000 | bytes 8000000 | tf_op jit(solution)/shard_map/pallas_call | solution.py:431
  60.5 1.0 %shard_map.95 = (bf16[1,128,512]{2,1,0:T(8,128)(2,1)}, f32[1,2048]{1,0:T(1,128)}, bf16[512,1024]{1,0:T(8,128)(2,1)}) custom-call(bf16[1,128,512]{2,1,0:T(8,128)(2,1)S(1)} %get-tuple-element.6.gi, f32[1,2048]{1,0:T(1,128)S(1)} %get-tuple-element.7.gw, bf16[512,1024]{1,0:T(8,128)(2,1)S(1)} %get-tuple-element.8.gt), custom_call_target="tpu_custom_call" | custom-call | tf_op jit(solution)/shard_map/pallas_call | solution.py:487
Async XLA Ops:
  1.3 0.7 %copy-start = (s32[1,1,2]{2,1,0:T(1,128)S(1)}, s32[1,1,2]{2,1,0:T(1,128)}, u32[]{:S(2)}) copy-start(s32[1,1,2]{2,1,0:T(1,128)} %qb.1) | copy-start | bytes 28

commit v3 on v2

--- a/solution.py
+++ b/solution.py
@@ -18,6 +18,9 @@
 (TILE, IDZ, WZ, WY, FILM, IDY, GOUT, ROWY, ROWZ, GWY, GWZ, GWX, HALO, PAIR, GID, GIX, EDGE) = range(17)
 INP, TAB = 17, 22
 CHANNELS = 27
+
+
+FARTHEST = {4: (2, 1, 3), 8: (4, 3, 5, 2, 6, 1, 7)}
 
 
 def iota(shape, dim):
@@ -48,16 +51,16 @@
 
 
 def kernel(
-    inp, whbm, tab, go, clip, part, qb, o_gi, o_gw, o_gt, w,
+    inp, whbm, tab, go, clip, part, qhbm, o_gi, o_gw, o_gt, w, qb,
     tsend, tg, idz, idy, wy, tabv, frs, frr, flm, xg, hx, xx, gov, gsend, gg, p01, wcat, pickt,
     gbuf, segs, c1r, yr, zr, gws, gwr, gz, gzr, gxs, gxr, pb, gis, gir, gi2, gix, esend, ed,
     ssem, rsem, lsem,
 ):
     z = lax.axis_index("dp")
     s = lax.axis_index("seq")
-    x = s // 16
-    y = (s // 2) % NY
-    c = s % 2
+    x = lax.div(s, 16)
+    y = lax.rem(lax.div(s, 2), NY)
+    c = lax.rem(s, 2)
     m = 2 * x + c
     side = 2 * c - 1
 
@@ -65,7 +68,7 @@
         return (zz, xx * 16 + yy * 2 + cc)
 
     def gpeer(i):
-        return at(z, i // 2, y, i % 2)
+        return at(z, lax.div(i, 2), y, lax.rem(i, 2))
 
     def ypeer(i):
         return at(z, x, i, c)
@@ -79,7 +82,7 @@
     sibling = at(z, x, y, 1 - c)
 
     def hpeer(i):
-        return at(z, i, (y + side + NY) % NY, 1 - c)
+        return at(z, i, lax.rem(y + side + NY, NY), 1 - c)
 
     def remote(src, dst, send, recv, dev):
         return pltpu.make_async_remote_copy(
@@ -96,9 +99,8 @@
         waiting[chan] = whole.wait_recv
 
     def spread(chan, me, peer, src, slot, whole, n=8):
-        @pl.loop(1, n)
-        def _(d):
-            i = (me + d) % n
+        for d in FARTHEST[n]:
+            i = lax.rem(me + d, n)
             remote(src(i), slot(me), chan, chan, peer(i)).start()
 
         watch(chan, whole)
@@ -107,21 +109,20 @@
         waiting.pop(chan)()
 
     def x_spread(base, src, slot, slots):
-        @pl.loop(1, NX)
-        def _(d):
-            remote(src, slot(x, c), base, base + d, xpeer((x + d) % NX)).start()
+        for d in FARTHEST[NX]:
+            remote(src, slot(x, c), base, base + d, xpeer(lax.rem(x + d, NX))).start()
 
         remote(src, slot(x, c), base, base, sibling).start()
         pending.append(remote(slots(4), slots(4), base, base, sibling).wait_send)
         waiting[base] = remote(slot(x, 1 - c), slot(x, 1 - c), base, base, sibling).wait_recv
         for d in range(1, NX):
-            mine = slot((x - d + NX) % NX, c)
+            mine = slot(lax.rem(x + NX - d, NX), c)
             waiting[base + d] = remote(mine, mine, base, base + d, sibling).wait_recv
 
     def x_hand_on(base, slot, slots):
-        for d in range(1, NX):
+        for d in (1, 3, 2):
             collect(base + d)
-            mine = slot((x - d + NX) % NX, c)
+            mine = slot(lax.rem(x + NX - d, NX), c)
             remote(mine, mine, base + 4, base + 4, sibling).start()
 
         watch(base + 4, slots(3))
@@ -134,15 +135,13 @@
 
     barrier = pltpu.get_barrier_semaphore()
 
-    @pl.loop(1, 8)
-    def _(d):
-        pl.semaphore_signal(barrier, inc=1, device_id=gpeer((m + d) % G), device_id_type=MESH)
-        pl.semaphore_signal(barrier, inc=1, device_id=zpeer((z + d) % NZ), device_id_type=MESH)
-        pl.semaphore_signal(barrier, inc=1, device_id=ypeer((y + d) % NY), device_id_type=MESH)
-
-    @pl.loop(0, NX)
-    def _(i):
+    for d in FARTHEST[8]:
+        pl.semaphore_signal(barrier, inc=1, device_id=zpeer(lax.rem(z + d, NZ)), device_id_type=MESH)
+        pl.semaphore_signal(barrier, inc=1, device_id=ypeer(lax.rem(y + d, NY)), device_id_type=MESH)
+    for i in range(NX):
         pl.semaphore_signal(barrier, inc=1, device_id=hpeer(i), device_id_type=MESH)
+    for d in FARTHEST[8]:
+        pl.semaphore_signal(barrier, inc=1, device_id=gpeer(lax.rem(m + d, G)), device_id_type=MESH)
 
     xcol = pl.multiple_of(x * LANES, LANES)
     scol = pl.multiple_of(C + x * LANES, LANES)
@@ -151,12 +150,14 @@
     get_scale = pltpu.make_async_copy(tab.at[:, pl.ds(xcol, LANES)], tabv.at[:, pl.ds(0, LANES)], lsem.at[2])
     get_shift = pltpu.make_async_copy(tab.at[:, pl.ds(scol, LANES)], tabv.at[:, pl.ds(LANES, LANES)], lsem.at[3])
     get_w = pltpu.make_async_copy(whbm, w, lsem.at[4])
-    for copy in (get_w, get_go, get_in, get_scale, get_shift):
+    get_qb = pltpu.make_async_copy(qhbm, qb, lsem.at[5])
+    for copy in (get_w, get_qb, get_go, get_in, get_scale, get_shift):
         copy.start()
 
     row8 = iota((8, LANES), 0)
     lane = iota((8, LANES), 1)
     info = jnp.where(lane == 0, part[0, 0], 0)
+    get_qb.wait()
     info = jnp.where(lane == 1, qb[0, 0, 0], info)
     info = jnp.where(lane == 2, qb[0, 0, 1], info)
     info = jnp.where(lane == 3, clip[0], info).astype(F32)
@@ -179,15 +180,7 @@
     def frame_slots(n):
         return xg.at[pl.ds(0, n)]
 
-    x_spread(INP, inp.at[0], frame_slot, frame_slots)
     turn = (c * ((y + 1) // NY) + (1 - c) * (3 * ((NY - y) // NY))) % NX
-
-    @pl.loop(0, NX)
-    def _(i):
-        src = inp.at[0, pl.ds(pl.multiple_of(c * 112, 16), 16), :]
-        remote(src, hx.at[(x + turn) % NX], HALO, HALO, hpeer(i)).start()
-
-    watch(HALO, hx)
 
     get_go.wait()
     ri, rj = iota((256, 256), 0), iota((256, 256), 1)
@@ -197,7 +190,6 @@
         qi, ci = i // 2, i % 2
         gsend[i] = gde[ci * ROWS : (ci + 1) * ROWS, qi * LANES : (qi + 1) * LANES]
     gg[m] = gsend[m]
-    spread(GOUT, m, gpeer, lambda i: gsend.at[i], lambda i: gg.at[i], gg.at[pl.ds(0, 7)])
 
     collect(TILE)
     rows_a = jnp.zeros((8, LANES), F32)
@@ -210,14 +202,22 @@
         ids = jnp.where(row8 == i, tile[2:3], ids)
     idz[z] = ids
     wy[y, z] = jnp.concatenate([rows_a, rows_b], 0).astype(BF16)
+    spread(WZ, z, zpeer, lambda i: wy.at[y, z], lambda i: wy.at[y, i], wy.at[y, pl.ds(0, 7)])
     spread(IDZ, z, zpeer, lambda i: idz.at[z], lambda i: idz.at[i], idz.at[pl.ds(0, 7)])
-    spread(WZ, z, zpeer, lambda i: wy.at[y, z], lambda i: wy.at[y, i], wy.at[y, pl.ds(0, 7)])
+    x_spread(INP, inp.at[0], frame_slot, frame_slots)
+    @pl.loop(0, NX)
+    def _(i):
+        src = inp.at[0, pl.ds(pl.multiple_of(c * 112, 16), 16), :]
+        remote(src, hx.at[(x + turn) % NX], HALO, HALO, hpeer(i)).start()
+
+    watch(HALO, hx)
+
+    spread(GOUT, m, gpeer, lambda i: gsend.at[i], lambda i: gg.at[i], gg.at[pl.ds(0, 7)])
 
     @pl.loop(0, 8)
     def _(b):
         row = b * LANES + iota((LANES, LANES), 0)
-        tap, chan = row // C, row % C
-        place = (chan // 2) % 8 * 128 + chan // 64 * 16 + tap * 8 + chan // 16 % 4 * 2 + chan % 2
+        place = ((row >> 1) & 7) * 128 + ((row >> 6) & 7) * 16 + (row >> 9) * 8 + ((row >> 4) & 3) * 2 + (row & 1)
         off = place - iota((LANES, LANES), 1)
         for k in range(8):
             p01[pl.ds(pl.multiple_of(b * LANES, LANES), LANES), k * LANES : (k + 1) * LANES] = jnp.where(
@@ -427,7 +427,7 @@
     hbm = pl.BlockSpec(memory_space=pltpu.HBM)
     smem = pl.BlockSpec(memory_space=pltpu.SMEM)
     V = pltpu.VMEM
-    large = [pltpu.with_memory_space_constraint(a, pltpu.HBM) for a in (inputs, weight, table, grad_out)]
+    large = [pltpu.with_memory_space_constraint(a, pltpu.HBM) for a in (inputs, weight, table, grad_out, quote_bounds)]
     outs = pl.pallas_call(
         kernel,
         out_shape=(
@@ -435,10 +435,11 @@
             jax.ShapeDtypeStruct(weight.shape, F32),
             jax.ShapeDtypeStruct(table.shape, BF16),
         ),
-        in_specs=[hbm] * 4 + [smem] * 3,
+        in_specs=[hbm] * 4 + [smem] * 2 + [hbm],
         out_specs=(vmem, vmem, vmem),
         scratch_shapes=[
             V((1, 4 * C), BF16),
+            pltpu.SMEM((1, 1, 2), jnp.int32),
             V((G, 8, LANES), F32),
             V((G, 8, LANES), F32),
             V((NZ, 8, LANES), F32),
@@ -477,13 +478,13 @@
             V((NX, 8, C), F32),
             pltpu.SemaphoreType.DMA((CHANNELS,)),
             pltpu.SemaphoreType.DMA((CHANNELS,)),
-            pltpu.SemaphoreType.DMA((5,)),
+            pltpu.SemaphoreType.DMA((6,)),
         ],
         compiler_params=pltpu.CompilerParams(
             collective_id=0, has_side_effects=True, vmem_limit_bytes=48 * 1024 * 1024
         ),
         cost_estimate=pl.CostEstimate(flops=2_000_000_000, bytes_accessed=8_000_000, transcendentals=131072),
-    )(*large, clip_speaker, part_speaker, quote_bounds)
+    )(*large[:4], clip_speaker, part_speaker, large[4])
     return pl.pallas_call(
         place,
         out_shape=[jax.ShapeDtypeStruct(o.shape, o.dtype) for o in outs],

time: 61.7 us -> 57.8 us (0.937)
  Pallas kernels: 59.5 us -> 55.8 us
    pallas_call x1, Pallas kernels: 58.5 us -> 54.7 us  [body(): pl.pallas_call(kernel, out_shape=(jax.ShapeDtypeStruct(inputs.shape, BF16...]
where the time goes in v3:
time: 57.8 us; the launch traced here: 57.7 us
  Pallas kernels  55.8 us (97%)
  between operations  1.93 us (3%)
    pallas_call x1, Pallas kernels, body(): pl.pallas_call(kernel, out_shape=(jax.ShapeDtypeStruct(inputs.shape, BF16...  54.7 us

profile of v3, /device:TPU:1, one launch (start us, length us, event | category | flops | bytes accessed | tf_op | source)
XLA Modules:
  0.0 57.7 jit_solution(13311947111572748023)
XLA Ops:
  1.9 54.7 %shard_map.94 = (bf16[1,128,512]{2,1,0:T(8,128)(2,1)S(1)}, f32[1,2048]{1,0:T(1,128)S(1)}, bf16[512,1024]{1,0:T(8,128)(2,1)S(1)}) custom-call(bf16[1,128,512]{2,1,0:T(8,128)(2,1)} %inp.1, bf16[1,2048]{1,0:T(2,128)(2,1)} %whbm.1, bf16[512,1024]{1,0:T(8,128)(2,1)} %tab.1, bf16[1,256,512]{2,1,0:T(8,128)(2,1)} %go.1, s32[1]{0:T(128)S(6)} %copy.10.clip, ...), custom_call_target="tpu_custom_call" | custom-call | flops 2000000000 | bytes 8000000 | tf_op jit(solution)/shard_map/pallas_call | solution.py:431
  56.7 1.0 %shard_map.95 = (bf16[1,128,512]{2,1,0:T(8,128)(2,1)}, f32[1,2048]{1,0:T(1,128)}, bf16[512,1024]{1,0:T(8,128)(2,1)}) custom-call(bf16[1,128,512]{2,1,0:T(8,128)(2,1)S(1)} %get-tuple-element.6.gi, f32[1,2048]{1,0:T(1,128)S(1)} %get-tuple-element.7.gw, bf16[512,1024]{1,0:T(8,128)(2,1)S(1)} %get-tuple-element.8.gt), custom_call_target="tpu_custom_call" | custom-call | tf_op jit(solution)/shard_map/pallas_call | solution.py:488

commit v4 on v3

--- a/solution.py
+++ b/solution.py
@@ -202,8 +202,8 @@
         ids = jnp.where(row8 == i, tile[2:3], ids)
     idz[z] = ids
     wy[y, z] = jnp.concatenate([rows_a, rows_b], 0).astype(BF16)
+    spread(IDZ, z, zpeer, lambda i: idz.at[z], lambda i: idz.at[i], idz.at[pl.ds(0, 7)])
     spread(WZ, z, zpeer, lambda i: wy.at[y, z], lambda i: wy.at[y, i], wy.at[y, pl.ds(0, 7)])
-    spread(IDZ, z, zpeer, lambda i: idz.at[z], lambda i: idz.at[i], idz.at[pl.ds(0, 7)])
     x_spread(INP, inp.at[0], frame_slot, frame_slots)
     @pl.loop(0, NX)
     def _(i):
@@ -239,7 +239,6 @@
         asked.append(jnp.where(clip_id - base == lane512, 1.0, 0.0))
         packed = jnp.where(lane == i, part_id, jnp.where(lane == 8 + i, clip_id, packed))
     idy[y] = packed
-    spread(IDY, y, ypeer, lambda i: idy.at[y], lambda i: idy.at[i], idy.at[pl.ds(0, 7)])
     get_scale.wait()
     get_shift.wait()
     served = dot(jnp.concatenate(asked, 0).astype(BF16), tabv[...]).astype(BF16)
@@ -247,6 +246,7 @@
         frs[i] = served[16 * i : 16 * (i + 1)]
     frr[z] = frs[z]
     spread(FILM, z, zpeer, lambda i: frs.at[i], lambda i: frr.at[i], frr.at[pl.ds(0, 7)])
+    spread(IDY, y, ypeer, lambda i: idy.at[y], lambda i: idy.at[i], idy.at[pl.ds(0, 7)])
 
     x_hand_on(INP, frame_slot, frame_slots)
     get_in.wait()

time: 57.8 us -> 58.5 us (1.012)
  Pallas kernels: 55.8 us -> 56.4 us
    pallas_call x1, Pallas kernels: 54.7 us -> 55.3 us  [body(): pl.pallas_call(kernel, out_shape=(jax.ShapeDtypeStruct(inputs.shape, BF16...]
where the time goes in v4:
time: 58.5 us; the launch traced here: 58.3 us
  Pallas kernels  56.4 us (96%)
  between operations  1.93 us (3%)
    pallas_call x1, Pallas kernels, body(): pl.pallas_call(kernel, out_shape=(jax.ShapeDtypeStruct(inputs.shape, BF16...  55.3 us

profile of v4, /device:TPU:1, one launch (start us, length us, event | category | flops | bytes accessed | tf_op | source)
XLA Modules:
  0.0 58.3 jit_solution(11957550664850874194)
XLA Ops:
  1.9 55.3 %shard_map.94 = (bf16[1,128,512]{2,1,0:T(8,128)(2,1)S(1)}, f32[1,2048]{1,0:T(1,128)S(1)}, bf16[512,1024]{1,0:T(8,128)(2,1)S(1)}) custom-call(bf16[1,128,512]{2,1,0:T(8,128)(2,1)} %inp.1, bf16[1,2048]{1,0:T(2,128)(2,1)} %whbm.1, bf16[512,1024]{1,0:T(8,128)(2,1)} %tab.1, bf16[1,256,512]{2,1,0:T(8,128)(2,1)} %go.1, s32[1]{0:T(128)S(6)} %copy.10.clip, ...), custom_call_target="tpu_custom_call" | custom-call | flops 2000000000 | bytes 8000000 | tf_op jit(solution)/shard_map/pallas_call | solution.py:431
  57.3 1.0 %shard_map.95 = (bf16[1,128,512]{2,1,0:T(8,128)(2,1)}, f32[1,2048]{1,0:T(1,128)}, bf16[512,1024]{1,0:T(8,128)(2,1)}) custom-call(bf16[1,128,512]{2,1,0:T(8,128)(2,1)S(1)} %get-tuple-element.6.gi, f32[1,2048]{1,0:T(1,128)S(1)} %get-tuple-element.7.gw, bf16[512,1024]{1,0:T(8,128)(2,1)S(1)} %get-tuple-element.8.gt), custom_call_target="tpu_custom_call" | custom-call | tf_op jit(solution)/shard_map/pallas_call | solution.py:488
